TPU v7x, 32 devices: a whole 2x2x4 slice. The times are simulated.
32 devices in a mesh: gx: 4 (over z), gy: 8 (over y, x, core).
Axes of the slice: x: 2, y: 2, z: 4, core: 2. Of those that a mesh axis runs over, the one named last changes fastest.
Arguments:
- enthalpy: float32 [64, 128, 1024], P(None, 'gx', 'gy'), may hold values from -6 to 6
- heat_cap: float32 [64, 128, 1024], P(None, 'gx', 'gy'), may hold values from 1 to 2
- conductivity: float32 [64, 128, 1024], P(None, 'gx', 'gy'), may hold values from 0.5 to 2
- phase: int32 [64, 128, 1024], P(None, 'gx', 'gy'), may hold values 0 or 1
- level_set: float32 [64, 128, 1024], P(None, 'gx', 'gy'), may hold values from -6 to 6
- band_flag: int32 [2, 4, 32], P(None, 'gx', 'gy'), may hold values from 0 to 1, as said below
Outputs:
- enthalpy_out: float32 [64, 128, 1024], P(None, 'gx', 'gy')
- level_out: float32 [64, 128, 1024], P(None, 'gx', 'gy')
Inputs may be any that keep to these rules, and one draw needn't show every extreme that they name: `band_flag`: two devices whose gy indices differ only in the lowest bit hold together exactly 4 band tiles among their tiles; for each gx index, at least one pair of gy indices (2k, 2k+1) has one device holding all 4 band tiles and its partner none.
All inputs are finite; a program needn't handle non-finite values. No bound on the sum of `phase` on one device may be relied on, other than what follows from the above.
Results may differ from a plain program's by a relative error of at most 0.0003.
Values sent between devices are 32-bit elements; how exact they have to be, the bound alone decides.
A program may use at most 128 MiB of HBM per device.

v0:
```python
import functools

import jax
import jax.numpy as jnp
from jax import lax
from jax.experimental import pallas as pl
from jax.experimental.pallas import tpu as pltpu
from jax.sharding import PartitionSpec as P

TILE = 32
DT_HEAT = 0.08
LATENT_HEAT = 1.5
GROWTH_RATE = 0.5
MELT_POINT = 0.25
DT_LEVEL = 0.25
WENO_FLOOR = 1e-06

OFF = 16
LO, HI = 0, 1
F32 = jnp.float32


def recip(value):
    guess = pl.reciprocal(value, approx=True)
    return guess * (2.0 - value * guess)


def weno(d0, d1, d2, d3, d4, d5):
    c0, c1, c2, c3, c4 = d1 - d0, d2 - d1, d3 - d2, d4 - d3, d5 - d4
    e1, e2, e3, e4 = c1 - c0, c2 - c1, c3 - c2, c4 - c3
    f1, f2, f3, f4 = [(13.0 / 3.0) * e * e + 4.0 * WENO_FLOOR for e in (e1, e2, e3, e4)]
    two1, two2, two3 = c1 + c1, c2 + c2, c3 + c3
    tri1, tri2, tri3 = two1 + c1, two2 + c2, two3 + c3

    def side(base, qa, qb, qc, na, nb, nc):
        ab, ac, bc = qa * qb, qa * qc, qb * qc
        wa, wb, wc = bc * bc, 6.0 * (ac * ac), 3.0 * (ab * ab)
        return base + (wa * na + wb * nb + wc * nc) * recip(6.0 * (wa + wb + wc))

    def sq(v):
        return v * v

    minus = side(
        d2, f1 + sq(two1 + e1), f2 + sq(c1 + c2), f3 + sq(two2 - e3),
        tri1 + (e1 + e1), c1 + two2, tri2 - e3,
    )
    plus_neg = side(
        -d3, f4 + sq(e4 - two3), f3 + sq(c2 + c3), f2 + sq(two2 + e2),
        tri3 - (e4 + e4), c3 + two2, tri2 + e2,
    )
    grow = jnp.maximum(jnp.maximum(minus, plus_neg), 0.0)
    fall = jnp.minimum(jnp.minimum(minus, plus_neg), 0.0)
    return grow * grow, fall * fall


def kernel(
    ngx, ngy, chunk,
    flag, enth, heat, cond, phase, level, eout, lout,
    lv, hl, sq, ua, ub, ihc, tm, ex, wsum, s0, hs0, s1, hs1, cx, ch, gs, rs,
    sx1, rx1, sy1, ry1, sxl, rxl, syl, ryl, sx2, rx2, sy2, ry2, sx3, rx3, sy3, ry3,
    send_sem, recv_sem,
):
    nz, nx, ny = enth.shape
    top = OFF + nx
    gx, gy = lax.axis_index("gx"), lax.axis_index("gy")
    west, east = lax.rem(gx + ngx - 1, ngx), lax.rem(gx + 1, ngx)
    south, north = lax.rem(gy + ngy - 1, ngy), lax.rem(gy + 1, ngy)
    others = [(a, b) for a in (west, gx, east) for b in (south, gy, north) if not (a is gx and b is gy)]
    barrier = pltpu.get_barrier_semaphore()
    for other in others:
        pl.semaphore_signal(barrier, inc=1, device_id=other, device_id_type=pl.DeviceIdType.MESH)

    lane = lax.broadcasted_iota(jnp.int32, (1, ny), 1)
    own = slice(OFF, top)
    count = [0]

    def copy(src, dst, where):
        i = count[0]
        count[0] += 1
        c = pltpu.make_async_remote_copy(
            src_ref=src, dst_ref=dst, send_sem=send_sem.at[i], recv_sem=recv_sem.at[i],
            device_id=where, device_id_type=pl.DeviceIdType.MESH,
        )
        c.start()
        return c

    def send_x(sx, rx):
        return [
            copy(sx.at[LO], rx.at[HI], (west, gy)),
            copy(sx.at[HI], rx.at[LO], (east, gy)),
        ]

    def send_y(sy, ry):
        return [copy(sy, ry.at[HI], (gx, south)), copy(sy, ry.at[LO], (gx, north))]

    def send_y_corners(sy, ry):
        out = []
        for side, where in ((HI, south), (LO, north)):
            r = ry.at[side]
            out.append(copy(sy, r.at[:, 8 : 8 + nx], (gx, where)))
            out.append(copy(sy.at[:, 0:8], r.at[:, 8 + nx : 16 + nx], (west, where)))
            out.append(copy(sy.at[:, nx - 8 : nx], r.at[:, 0:8], (east, where)))
        return out

    def up(x, h, k=1):
        return pltpu.roll(jnp.where(lane < k, h, x), ny - k, 1)

    def down(x, h, k=1):
        return pltpu.roll(jnp.where(lane >= ny - k, h, x), k, 1)

    def pack(x, z, width, acc):
        group = ny // (2 * width)
        g = lax.rem(z, group)
        return jnp.where(lane // (2 * width) == g, pltpu.roll(x, g * (2 * width) + width, 1), acc)

    def unpack(packed, z, width):
        group = ny // (2 * width)
        g = lax.rem(z, group)
        return pltpu.roll(packed, ny - (g * (2 * width) + width), 1)

    def merged(from_lo, from_hi, width):
        return jnp.where(lane % (2 * width) >= width, from_hi, from_lo)

    def rows_of(ref, row):
        rows = ref.shape[1]
        return ref.reshape(ref.shape[0] * rows, ny), rows, row

    def get_row(ref, row, z0=0):
        flat, rows, row = rows_of(ref, row)
        return flat[pl.ds(z0 * rows + row, nz, stride=rows), :]

    def put_row(ref, row, value, z0=0):
        flat, rows, row = rows_of(ref, row)
        flat[pl.ds(z0 * rows + row, nz, stride=rows), :] = value

    def start(z, acc):
        accu, accs = acc
        e = enth[z] - LATENT_HEAT * phase[z].astype(F32)
        r = 1.0 / heat[z]
        t = e * r
        s = jnp.sqrt(cond[z])
        u = s * t
        ihc[z], tm[z], ex[z] = r, t, e
        sq[z, own], ua[z, own] = s, u
        return pack(u, z, 1, accu), pack(s, z, 1, accs)

    zero = jnp.zeros((nx, ny), F32)
    sy1[0], sy1[1] = lax.fori_loop(0, nz, start, (zero, zero))
    for i, ref in enumerate((ua, sq)):
        sx1[LO, i] = get_row(ref, OFF)
        sx1[HI, i] = get_row(ref, top - 1)
    pl.semaphore_wait(barrier, len(others))
    first = send_x(sx1, rx1) + send_y(sy1, ry1)

    def level_group(q, _):
        def one(g, acc):
            z = q * 16 + g
            x = level[z]
            lv[z + 3, own] = x
            return pack(x, z, 4, acc)

        syl[q] = lax.fori_loop(0, 16, one, zero)
        return 0

    lax.fori_loop(0, nz // 16, level_group, 0)
    for k in range(3):
        sxl[LO, k] = get_row(lv, OFF + k, 3)
        sxl[HI, k] = get_row(lv, top - 3 + k, 3)
    levels = send_x(sxl, rxl) + send_y_corners(syl, ryl)

    def ends(ref, rows):
        for k in range(3):
            ref[k, rows] = ref[3, rows]
            ref[nz + 3 + k, rows] = ref[nz + 2, rows]

    ends(lv, own)

    def weno_z(z, _):
        for r in range(0, nx, chunk):
            at = slice(OFF + r, OFF + r + chunk)
            v = [lv[z + k, at] for k in range(7)]
            g, f = weno(*[v[k + 1] - v[k] for k in range(6)])
            gs[z, r : r + chunk], rs[z, r : r + chunk] = g, f
        return 0

    lax.fori_loop(0, nz, weno_z, 0)

    def around(ref, z, packed):
        x = ref[z, own]
        h = unpack(packed, z, 1)
        return (
            ref[jnp.maximum(z - 1, 0), own] + ref[jnp.minimum(z + 1, nz - 1), own]
            + (ref[z, OFF - 1 : top - 1] + ref[z, OFF + 1 : top + 1])
            + (up(x, h) + down(x, h))
        )

    for c in first:
        c.wait()
    for i, ref in enumerate((ua, sq)):
        put_row(ref, OFF - 1, rx1[LO, i])
        put_row(ref, top, rx1[HI, i])

    def substep1(z, acc):
        pu = merged(ry1[LO, 0], ry1[HI, 0], 1)
        ps = merged(ry1[LO, 1], ry1[HI, 1], 1)
        w = around(sq, z, ps)
        s = sq[z, own]
        e = ex[z] + DT_HEAT * (s * (around(ua, z, pu) - tm[z] * w))
        t = e * ihc[z]
        u = s * t
        wsum[z], ex[z], tm[z], ub[z, own] = w, e, t, u
        return pack(u, z, 1, acc)

    sy2[...] = lax.fori_loop(0, nz, substep1, zero)
    sx2[LO] = get_row(ub, OFF)
    sx2[HI] = get_row(ub, top - 1)
    second = send_x(sx2, rx2) + send_y(sy2, ry2)

    for c in levels:
        c.wait()
    for k in range(3):
        put_row(lv, OFF - 3 + k, rxl[LO, k], 3)
        put_row(lv, top + k, rxl[HI, k], 3)
    wide = slice(OFF - 8, top + 8)

    def level_halo(z, _):
        q = z // 16
        hl[z + 3, wide] = unpack(merged(ryl[LO, q], ryl[HI, q], 4), z, 4)
        return 0

    lax.fori_loop(0, nz, level_halo, 0)
    ends(lv, wide)
    ends(hl, wide)

    def weno_xy(z, _):
        half = z // TILE
        masks = [jnp.where(flag[half, 0, j] == 1, -DT_LEVEL, 0.0) for j in range(ny // TILE)]
        mask = jnp.full((1, ny), masks[0])
        for j in range(1, ny // TILE):
            mask = jnp.where(lane >= j * TILE, masks[j], mask)
        for r in range(0, nx, chunk):
            a = OFF + r
            x = lv[z + 3, a : a + chunk]
            v = [x if k == 3 else lv[z + 3, a + k - 3 : a + k - 3 + chunk] for k in range(7)]
            g1, f1 = weno(*[v[k + 1] - v[k] for k in range(6)])
            h = hl[z + 3, a : a + chunk]
            v = [down(x, h, k) for k in (3, 2, 1)] + [x] + [up(x, h, k) for k in (1, 2, 3)]
            g2, f2 = weno(*[v[k + 1] - v[k] for k in range(6)])
            at = slice(r, r + chunk)
            gs[z, at] = mask * jnp.sqrt(gs[z, at] + g1 + g2 + 1e-06)
            rs[z, at] = mask * jnp.sqrt(rs[z, at] + f1 + f2 + 1e-06)
        return 0

    def coefs(out, oz, orow, main, side, z, a, rows):
        at = slice(a, a + rows)
        x, h = main[z + 3, at], side[z + 3, at]
        d0 = main[z + 4, at] - main[z + 2, at]
        d1 = main[z + 3, a + 1 : a + 1 + rows] - main[z + 3, a - 1 : a - 1 + rows]
        d2 = up(x, h) - down(x, h)
        d0, d1, d2 = d0 * d0, d1 * d1, d2 * d2
        total = d0 + d1 + d2
        inv = recip(4.0 + 3.0 * total)
        to = slice(orow, orow + rows)
        out[0, oz, to] = (4.0 + total) * inv
        out[1, oz, to] = d0 * inv
        out[2, oz, to] = d1 * inv
        out[3, oz, to] = d2 * inv

    def coefs_x(i, _):
        coefs(cx, i, 0, lv, hl, i - 1, OFF - 8, nx + 16)
        return 0

    def coefs_h(z, _):
        coefs(ch, z, 0, hl, lv, z, OFF, nx)
        return 0

    lax.fori_loop(0, nz // 2, weno_xy, 0)

    for c in second:
        c.wait()
    put_row(ub, OFF - 1, rx2[LO])
    put_row(ub, top, rx2[HI])

    def substep2_group(q, _):
        def substep2(g, acc):
            z = q * 32 + g
            pu = merged(ry2[LO], ry2[HI], 1)
            e = ex[z] + DT_HEAT * (sq[z, own] * (around(ub, z, pu) - tm[z] * wsum[z]))
            eout[z] = e + LATENT_HEAT * phase[z].astype(F32)
            s = GROWTH_RATE * (MELT_POINT - e * ihc[z])
            s0[z, own] = s
            return pack(s, z, 2, acc)

        sy3[q] = lax.fori_loop(0, 32, substep2, zero)
        return 0

    lax.fori_loop(0, nz // 32, substep2_group, 0)
    for k in range(2):
        sx3[LO, k] = get_row(s0, OFF + k)
        sx3[HI, k] = get_row(s0, top - 2 + k)
    third = send_x(sx3, rx3) + send_y_corners(sy3, ry3)

    lax.fori_loop(nz // 2, nz, weno_xy, 0)
    lax.fori_loop(0, nz + 2, coefs_x, 0)
    lax.fori_loop(0, nz, coefs_h, 0)

    for c in third:
        c.wait()
    for k in range(2):
        put_row(s0, OFF - 2 + k, rx3[LO, k])
        put_row(s0, top + k, rx3[HI, k])

    def speed_halo(z, _):
        q = z // 32
        hs0[z, wide] = unpack(merged(ry3[LO, q], ry3[HI, q], 2), z, 2)
        return 0

    lax.fori_loop(0, nz, speed_halo, 0)

    def clamp(z):
        return jnp.minimum(jnp.maximum(z, 0), nz - 1)

    def sweep(c, cz, crow, main, zb, zc, za, side, a, rows):
        at, to = slice(a, a + rows), slice(crow, crow + rows)
        x = main[zc, at]
        return (
            c[0, cz, to] * x
            + c[1, cz, to] * (main[zb, at] + main[za, at])
            + c[2, cz, to] * (main[zc, a - 1 : a - 1 + rows] + main[zc, a + 1 : a + 1 + rows])
            + c[3, cz, to] * (up(x, side) + down(x, side))
        )

    def sweep1_x(i, _):
        b, m, t = clamp(i - 2), clamp(i - 1), clamp(i)
        s1[i, wide] = sweep(cx, i, 0, s0, b, m, t, hs0[m, wide], OFF - 8, nx + 16)
        return 0

    lax.fori_loop(0, nz + 2, sweep1_x, 0)

    def sweep1_h(z, _):
        hs1[z] = sweep(ch, z, 0, hs0, clamp(z - 1), z, clamp(z + 1), s0[z, own], OFF, nx)
        return 0

    lax.fori_loop(0, nz, sweep1_h, 0)

    def last(z, _):
        s = sweep(cx, z + 1, 8, s1, z, z + 1, z + 2, hs1[z], OFF, nx)
        lout[z] = level[z] + s * jnp.where(s >= 0.0, gs[z], rs[z])
        return 0

    lax.fori_loop(0, nz, last, 0)


CHUNK = 16


def body(ngx, ngy, enthalpy, heat_cap, conductivity, phase, level_set, band_flag):
    nz, nx, ny = enthalpy.shape
    tall = nx + 2 * OFF

    def vmem(*shape):
        return pltpu.VMEM(shape, F32)

    copies = 4 + 8 + 4 + 8
    scratch = [
        vmem(nz + 6, tall, ny),
        vmem(nz + 6, tall, ny),
        vmem(nz, tall, ny),
        vmem(nz, tall, ny),
        vmem(nz, tall, ny),
        vmem(nz, nx, ny),
        vmem(nz, nx, ny),
        vmem(nz, nx, ny),
        vmem(nz, nx, ny),
        vmem(nz, tall, ny),
        vmem(nz, tall, ny),
        vmem(nz + 2, tall, ny),
        vmem(nz, nx, ny),
        vmem(4, nz + 2, nx + 16, ny),
        vmem(4, nz, nx, ny),
        vmem(nz, nx, ny),
        vmem(nz, nx, ny),
        vmem(2, 2, nz, ny), vmem(2, 2, nz, ny), vmem(2, nx, ny), vmem(2, 2, nx, ny),
        vmem(2, 3, nz, ny), vmem(2, 3, nz, ny), vmem(nz // 16, nx, ny), vmem(2, nz // 16, nx + 16, ny),
        vmem(2, nz, ny), vmem(2, nz, ny), vmem(nx, ny), vmem(2, nx, ny),
        vmem(2, 2, nz, ny), vmem(2, 2, nz, ny), vmem(nz // 32, nx, ny), vmem(2, nz // 32, nx + 16, ny),
        pltpu.SemaphoreType.DMA((copies,)),
        pltpu.SemaphoreType.DMA((copies,)),
    ]
    whole = pl.BlockSpec(memory_space=pltpu.VMEM)
    out = jax.ShapeDtypeStruct((nz, nx, ny), F32)
    return pl.pallas_call(
        functools.partial(kernel, ngx, ngy, CHUNK),
        out_shape=(out, out),
        in_specs=[pl.BlockSpec(memory_space=pltpu.SMEM)] + [whole] * 5,
        out_specs=(whole, whole),
        scratch_shapes=scratch,
        compiler_params=pltpu.CompilerParams(
            collective_id=0, has_side_effects=True, vmem_limit_bytes=60 * 1024 * 1024
        ),
    )(band_flag, enthalpy, heat_cap, conductivity, phase, level_set)


def solution(mesh):
    spec = P(None, "gx", "gy")
    return jax.shard_map(
        functools.partial(body, mesh.shape["gx"], mesh.shape["gy"]),
        mesh=mesh, in_specs=(spec,) * 6, out_specs=(spec, spec), check_vma=False,
    )
```

profile of v0, /device:TPU:0, one launch (start us, length us, event | category | flops | bytes accessed | tf_op | source)
XLA Modules:
  0.0 103.6 jit_solution(13765485732508064136)
XLA Ops:
  0.6 99.7 %shard_map.77 = (f32[64,32,128]{2,1,0:T(8,128)}, f32[64,32,128]{2,1,0:T(8,128)}) custom-call(s32[2,1,4]{2,1,0:T(1,128)} %flag.1, f32[64,32,128]{2,1,0:T(8,128)} %enth.1, f32[64,32,128]{2,1,0:T(8,128)} %heat.1, f32[64,32,128]{2,1,0:T(8,128)} %cond.1, s32[64,32,128]{2,1,0:T(8,128)} %phase.1, f32[64,32,128]{2,1,0:T(8,128)} %level.1), custom_call_target="tpu_custom_call" | custom-call | tf_op jit(solution)/shard_map/pallas_call | solution.py:392
  100.3 0.0 copy-start
  100.3 2.4 %copy.10 = f32[64,32,128]{2,1,0:T(8,128)} copy(f32[64,32,128]{2,1,0:T(8,128)} %get-tuple-element.4) | data formatting | bytes 2097152
  102.7 0.0 copy-done
  102.7 1.0 copy.11
Async XLA Ops:
  100.3 2.4 %copy-start = (f32[64,32,128]{2,1,0:T(8,128)S(1)}, f32[64,32,128]{2,1,0:T(8,128)}, u32[]{:S(2)}) copy-start(f32[64,32,128]{2,1,0:T(8,128)} %get-tuple-element.5) | copy-start | bytes 3145732
where the time goes:
time: 104 us
  Pallas kernels  99.7 us (96%)
  local copies, waits for them, and re-layouts  3.32 us (3%)
    pallas_call x1, Pallas kernels, body(): pl.pallas_call(functools.partial(kernel, ngx, ngy, CHUNK), out_shape=(out...  99.7 us
    unnamed x4, local copies, waits for them, and re-layouts  3.32 us

commit v1 on v0

--- a/solution.py
+++ b/solution.py
@@ -17,12 +17,27 @@
 
 OFF = 16
 LO, HI = 0, 1
+U_START, U_SUB, U_COEF, U_SWEEP, U_LAST, U_WENO = 8, 8, 8, 8, 8, 2
 F32 = jnp.float32
 
 
 def recip(value):
     guess = pl.reciprocal(value, approx=True)
     return guess * (2.0 - value * guess)
+
+
+def loop(low, high, step, init, unroll):
+    whole = (high - low) // unroll
+
+    def several(i, value):
+        for j in range(unroll):
+            value = step(low + i * unroll + j, value)
+        return value
+
+    value = lax.fori_loop(0, whole, several, init)
+    for i in range(low + whole * unroll, high):
+        value = step(i, value)
+    return value
 
 
 def weno(d0, d1, d2, d3, d4, d5):
@@ -145,7 +160,7 @@
         return pack(u, z, 1, accu), pack(s, z, 1, accs)
 
     zero = jnp.zeros((nx, ny), F32)
-    sy1[0], sy1[1] = lax.fori_loop(0, nz, start, (zero, zero))
+    sy1[0], sy1[1] = loop(0, nz, start, (zero, zero), U_START)
     for i, ref in enumerate((ua, sq)):
         sx1[LO, i] = get_row(ref, OFF)
         sx1[HI, i] = get_row(ref, top - 1)
@@ -159,7 +174,7 @@
             lv[z + 3, own] = x
             return pack(x, z, 4, acc)
 
-        syl[q] = lax.fori_loop(0, 16, one, zero)
+        syl[q] = loop(0, 16, one, zero, 16)
         return 0
 
     lax.fori_loop(0, nz // 16, level_group, 0)
@@ -183,7 +198,7 @@
             gs[z, r : r + chunk], rs[z, r : r + chunk] = g, f
         return 0
 
-    lax.fori_loop(0, nz, weno_z, 0)
+    loop(0, nz, weno_z, 0, U_WENO)
 
     def around(ref, z, packed):
         x = ref[z, own]
@@ -211,7 +226,7 @@
         wsum[z], ex[z], tm[z], ub[z, own] = w, e, t, u
         return pack(u, z, 1, acc)
 
-    sy2[...] = lax.fori_loop(0, nz, substep1, zero)
+    sy2[...] = loop(0, nz, substep1, zero, U_SUB)
     sx2[LO] = get_row(ub, OFF)
     sx2[HI] = get_row(ub, top - 1)
     second = send_x(sx2, rx2) + send_y(sy2, ry2)
@@ -228,7 +243,7 @@
         hl[z + 3, wide] = unpack(merged(ryl[LO, q], ryl[HI, q], 4), z, 4)
         return 0
 
-    lax.fori_loop(0, nz, level_halo, 0)
+    loop(0, nz, level_halo, 0, 8)
     ends(lv, wide)
     ends(hl, wide)
 
@@ -274,7 +289,7 @@
         coefs(ch, z, 0, hl, lv, z, OFF, nx)
         return 0
 
-    lax.fori_loop(0, nz // 2, weno_xy, 0)
+    loop(0, nz // 2, weno_xy, 0, U_WENO)
 
     for c in second:
         c.wait()
@@ -291,7 +306,7 @@
             s0[z, own] = s
             return pack(s, z, 2, acc)
 
-        sy3[q] = lax.fori_loop(0, 32, substep2, zero)
+        sy3[q] = loop(0, 32, substep2, zero, U_SUB)
         return 0
 
     lax.fori_loop(0, nz // 32, substep2_group, 0)
@@ -300,9 +315,9 @@
         sx3[HI, k] = get_row(s0, top - 2 + k)
     third = send_x(sx3, rx3) + send_y_corners(sy3, ry3)
 
-    lax.fori_loop(nz // 2, nz, weno_xy, 0)
-    lax.fori_loop(0, nz + 2, coefs_x, 0)
-    lax.fori_loop(0, nz, coefs_h, 0)
+    loop(nz // 2, nz, weno_xy, 0, U_WENO)
+    loop(0, nz + 2, coefs_x, 0, U_COEF)
+    loop(0, nz, coefs_h, 0, U_COEF)
 
     for c in third:
         c.wait()
@@ -315,7 +330,7 @@
         hs0[z, wide] = unpack(merged(ry3[LO, q], ry3[HI, q], 2), z, 2)
         return 0
 
-    lax.fori_loop(0, nz, speed_halo, 0)
+    loop(0, nz, speed_halo, 0, 8)
 
     def clamp(z):
         return jnp.minimum(jnp.maximum(z, 0), nz - 1)
@@ -335,20 +350,20 @@
         s1[i, wide] = sweep(cx, i, 0, s0, b, m, t, hs0[m, wide], OFF - 8, nx + 16)
         return 0
 
-    lax.fori_loop(0, nz + 2, sweep1_x, 0)
+    loop(0, nz + 2, sweep1_x, 0, U_SWEEP)
 
     def sweep1_h(z, _):
         hs1[z] = sweep(ch, z, 0, hs0, clamp(z - 1), z, clamp(z + 1), s0[z, own], OFF, nx)
         return 0
 
-    lax.fori_loop(0, nz, sweep1_h, 0)
+    loop(0, nz, sweep1_h, 0, U_SWEEP)
 
     def last(z, _):
         s = sweep(cx, z + 1, 8, s1, z, z + 1, z + 2, hs1[z], OFF, nx)
         lout[z] = level[z] + s * jnp.where(s >= 0.0, gs[z], rs[z])
         return 0
 
-    lax.fori_loop(0, nz, last, 0)
+    loop(0, nz, last, 0, U_LAST)
 
 
 CHUNK = 16

time: 104 us -> 45.9 us (0.44)
  Pallas kernels: 99.7 us -> 41.8 us
    pallas_call x1, Pallas kernels: 99.7 us -> 41.8 us  [body(): pl.pallas_call(functools.partial(kernel, ngx, ngy, CHUNK), out_shape=(out...]
where the time goes in v1:
time: 45.9 us; the launch traced here: 45.8 us
  Pallas kernels  41.8 us (91%)
  local copies, waits for them, and re-layouts  3.32 us (7%)
  between operations  0.65 us (1%)
    pallas_call x1, Pallas kernels, body(): pl.pallas_call(functools.partial(kernel, ngx, ngy, CHUNK), out_shape=(out...  41.8 us
    unnamed x4, local copies, waits for them, and re-layouts  3.32 us

profile of v1, /device:TPU:0, one launch (start us, length us, event | category | flops | bytes accessed | tf_op | source)
XLA Modules:
  0.0 45.8 jit_solution(8719171399303696509)
XLA Ops:
  0.6 41.8 %shard_map.77 = (f32[64,32,128]{2,1,0:T(8,128)}, f32[64,32,128]{2,1,0:T(8,128)}) custom-call(s32[2,1,4]{2,1,0:T(1,128)} %flag.1, f32[64,32,128]{2,1,0:T(8,128)} %enth.1, f32[64,32,128]{2,1,0:T(8,128)} %heat.1, f32[64,32,128]{2,1,0:T(8,128)} %cond.1, s32[64,32,128]{2,1,0:T(8,128)} %phase.1, f32[64,32,128]{2,1,0:T(8,128)} %level.1), custom_call_target="tpu_custom_call" | custom-call | tf_op jit(solution)/shard_map/pallas_call | solution.py:407
  42.4 0.0 copy-start
  42.4 2.4 %copy.10 = f32[64,32,128]{2,1,0:T(8,128)} copy(f32[64,32,128]{2,1,0:T(8,128)} %get-tuple-element.4) | data formatting | bytes 2097152
  44.8 0.0 copy-done
  44.8 1.0 %copy.11 = f32[64,32,128]{2,1,0:T(8,128)} copy(f32[64,32,128]{2,1,0:T(8,128)S(1)} %copy-done) | data formatting | bytes 2097152
Async XLA Ops:
  42.4 2.4 %copy-start = (f32[64,32,128]{2,1,0:T(8,128)S(1)}, f32[64,32,128]{2,1,0:T(8,128)}, u32[]{:S(2)}) copy-start(f32[64,32,128]{2,1,0:T(8,128)} %get-tuple-element.5) | copy-start | bytes 3145732

commit v2 on v1

--- a/solution.py
+++ b/solution.py
@@ -17,7 +17,7 @@
 
 OFF = 16
 LO, HI = 0, 1
-U_START, U_SUB, U_COEF, U_SWEEP, U_LAST, U_WENO = 8, 8, 8, 8, 8, 2
+U_START, U_SUB, U_COEF, U_SWEEP, U_LAST, U_WENO = 8, 8, 8, 8, 8, 4
 F32 = jnp.float32
 
 
@@ -215,9 +215,10 @@
         put_row(ref, OFF - 1, rx1[LO, i])
         put_row(ref, top, rx1[HI, i])
 
+    pu = merged(ry1[LO, 0], ry1[HI, 0], 1)
+    ps = merged(ry1[LO, 1], ry1[HI, 1], 1)
+
     def substep1(z, acc):
-        pu = merged(ry1[LO, 0], ry1[HI, 0], 1)
-        ps = merged(ry1[LO, 1], ry1[HI, 1], 1)
         w = around(sq, z, ps)
         s = sq[z, own]
         e = ex[z] + DT_HEAT * (s * (around(ua, z, pu) - tm[z] * w))
@@ -296,11 +297,12 @@
     put_row(ub, OFF - 1, rx2[LO])
     put_row(ub, top, rx2[HI])
 
+    pu2 = merged(ry2[LO], ry2[HI], 1)
+
     def substep2_group(q, _):
         def substep2(g, acc):
             z = q * 32 + g
-            pu = merged(ry2[LO], ry2[HI], 1)
-            e = ex[z] + DT_HEAT * (sq[z, own] * (around(ub, z, pu) - tm[z] * wsum[z]))
+            e = ex[z] + DT_HEAT * (sq[z, own] * (around(ub, z, pu2) - tm[z] * wsum[z]))
             eout[z] = e + LATENT_HEAT * phase[z].astype(F32)
             s = GROWTH_RATE * (MELT_POINT - e * ihc[z])
             s0[z, own] = s

time: 45.9 us -> 45.3 us (0.987)
  Pallas kernels: 41.8 us -> 41.1 us
    pallas_call x1, Pallas kernels: 41.8 us -> 41.1 us  [body(): pl.pallas_call(functools.partial(kernel, ngx, ngy, CHUNK), out_shape=(out...]
where the time goes in v2:
time: 45.3 us; the launch traced here: 45.1 us
  Pallas kernels  41.1 us (91%)
  local copies, waits for them, and re-layouts  3.32 us (7%)
  between operations  0.65 us (1%)
    pallas_call x1, Pallas kernels, body(): pl.pallas_call(functools.partial(kernel, ngx, ngy, CHUNK), out_shape=(out...  41.1 us
    unnamed x4, local copies, waits for them, and re-layouts  3.32 us

profile of v2, /device:TPU:0, one launch (start us, length us, event | category | flops | bytes accessed | tf_op | source)
XLA Modules:
  0.0 45.1 jit_solution(14142181788961895050)
XLA Ops:
  0.6 41.1 %shard_map.77 = (f32[64,32,128]{2,1,0:T(8,128)}, f32[64,32,128]{2,1,0:T(8,128)}) custom-call(s32[2,1,4]{2,1,0:T(1,128)} %flag.1, f32[64,32,128]{2,1,0:T(8,128)} %enth.1, f32[64,32,128]{2,1,0:T(8,128)} %heat.1, f32[64,32,128]{2,1,0:T(8,128)} %cond.1, s32[64,32,128]{2,1,0:T(8,128)} %phase.1, f32[64,32,128]{2,1,0:T(8,128)} %level.1), custom_call_target="tpu_custom_call" | custom-call | tf_op jit(solution)/shard_map/pallas_call | solution.py:409
  41.8 0.0 copy-start
  41.8 2.4 %copy.10 = f32[64,32,128]{2,1,0:T(8,128)} copy(f32[64,32,128]{2,1,0:T(8,128)} %get-tuple-element.4) | data formatting | bytes 2097152
  44.1 0.0 copy-done
  44.2 1.0 %copy.11 = f32[64,32,128]{2,1,0:T(8,128)} copy(f32[64,32,128]{2,1,0:T(8,128)S(1)} %copy-done) | data formatting | bytes 2097152
Async XLA Ops:
  41.8 2.4 %copy-start = (f32[64,32,128]{2,1,0:T(8,128)S(1)}, f32[64,32,128]{2,1,0:T(8,128)}, u32[]{:S(2)}) copy-start(f32[64,32,128]{2,1,0:T(8,128)} %get-tuple-element.5) | copy-start | bytes 3145732
